TPU v7x, 512 devices: a whole 4x8x8 slice. The times are simulated.
512 devices in a mesh: leaf: 32 (over y, x), row: 8 (over z), col: 2 (over core).
Axes of the slice: x: 4, y: 8, z: 8, core: 2. Of those that a mesh axis runs over, the one named last changes fastest.
Arguments:
- leaf_update: float32 [32, 512, 512], P('leaf', 'row', 'col'), as said below
- leaf_rhs: float32 [32, 512, 256], P('leaf', 'row', 'col'), may hold values from -6 to 6
- child_rows: int32 [31, 2, 512], replicated, may hold values from 0 to 1023, as said below
- separator_coef: float32 [31, 512], replicated, may hold values from 0.5 to 4
Outputs:
- final_update: float32 [512, 512], P('row', 'col')
- final_rhs: float32 [512, 256], P('row', 'col')
- separator_solutions: float32 [32, 512, 256], P('leaf', 'row', 'col')
Inputs may be any that keep to these rules, and one draw needn't show every extreme that they name: Each child_rows[f, c] lists 512 distinct rows of the front. Each leaf_update[i] is symmetric positive definite.
All inputs are finite; a program needn't handle non-finite values.
Results may differ from a plain program's by a relative error of at most 0.00017.
Values sent between devices are 32-bit elements; how exact they have to be, the bound alone decides.
A program may use at most 128 MiB of HBM per device.

v0:
```python
import jax
import jax.numpy as jnp
from jax import lax
from jax.sharding import PartitionSpec as P


def from_partner(block, axis, apart):
    count = lax.axis_size(axis)
    route = []
    for low in range(count):
        high = low | 1 << apart
        if high != low and high < count:
            route += [(low, high), (high, low)]
    return lax.ppermute(block, axis, route)


def stencil_block(sep_coefs):
    positions = jnp.arange(sep_coefs.shape[0], dtype=jnp.int32)
    distance = positions[:, None] - positions[None, :]
    return jnp.where(
        distance == 0, sep_coefs[:, None] + 2.0, jnp.where(jnp.abs(distance) == 1, -1.0, 0.0)
    )


def matmul_high(left, right):
    return jnp.dot(left, right, precision=lax.Precision.HIGHEST)


def factor_inverse(matrix):
    order = matrix.shape[0]
    if order <= 32:
        lower_factor = jnp.linalg.cholesky(matrix)
        identity = jnp.eye(order, dtype=matrix.dtype)
        return jax.scipy.linalg.solve_triangular(lower_factor, identity, lower=True)
    half = order // 2
    inv_top = factor_inverse(matrix[:half, :half])
    lower_left = matmul_high(matrix[half:, :half], inv_top.T)
    schur_part = matrix[half:, half:] - matmul_high(lower_left, lower_left.T)
    inv_bottom = factor_inverse(schur_part)
    inv_left = -matmul_high(inv_bottom, matmul_high(lower_left, inv_top))
    upper_rows = jnp.concatenate([inv_top, jnp.zeros((half, order - half), matrix.dtype)], axis=1)
    lower_rows = jnp.concatenate([inv_left, inv_bottom], axis=1)
    return jnp.concatenate([upper_rows, lower_rows], axis=0)


def inverse_map(mapping, front_size):
    sources = jnp.arange(mapping.shape[0], dtype=jnp.int32)
    return jnp.full((front_size,), -1, jnp.int32).at[mapping].set(sources)


def spread_rows(full_rows, inverse, parent_rows):
    source = inverse[parent_rows]
    present = source >= 0
    picked = jnp.take(full_rows, jnp.maximum(source, 0), axis=0)
    return jnp.where(present[:, None], picked, 0.0)


def spread_block(full_matrix, inverse, parent_rows, parent_cols):
    src_rows = inverse[parent_rows]
    src_cols = inverse[parent_cols]
    picked = jnp.take(
        jnp.take(full_matrix, jnp.maximum(src_rows, 0), axis=0), jnp.maximum(src_cols, 0), axis=1
    )
    present = (src_rows >= 0)[:, None] & (src_cols >= 0)[None, :]
    return jnp.where(present, picked, 0.0)


def per_device(leaf_update, leaf_rhs, child_rows, separator_coef):
    update_blk = leaf_update[0]
    rhs_blk = leaf_rhs[0]
    leaf_count = lax.axis_size("leaf")
    row_count = lax.axis_size("row")
    col_count = lax.axis_size("col")
    levels = leaf_count.bit_length() - 1
    leaf_index = lax.axis_index("leaf")
    row_index = lax.axis_index("row")
    col_index = lax.axis_index("col")
    row_block, col_block = update_blk.shape
    rhs_cols = rhs_blk.shape[1]
    update_size = row_block * row_count
    sep_size = separator_coef.shape[1]
    front_size = sep_size + update_size
    sep_rows = jnp.arange(sep_size, dtype=jnp.int32)
    own_rows = sep_size + row_index * row_block + jnp.arange(row_block, dtype=jnp.int32)
    own_cols = sep_size + col_index * col_block + jnp.arange(col_block, dtype=jnp.int32)
    sep_share = sep_size // row_count
    kept_rows = jnp.zeros((sep_share, rhs_cols), jnp.float32)
    offset = 0
    for level_no in range(1, levels + 1):
        bit_no = level_no - 1
        other_upd, other_rhs = from_partner((update_blk, rhs_blk), "leaf", bit_no)
        blocks = lax.all_gather(
            jnp.stack([update_blk, other_upd])[:, None], ("row", "col"), axis=1, tiled=True
        )
        whole_rhs = lax.all_gather(jnp.stack([rhs_blk, other_rhs]), "row", axis=1, tiled=True)
        whole_upd = (
            blocks.reshape(2, row_count, col_count, row_block, col_block)
            .transpose(0, 1, 3, 2, 4)
            .reshape(2, update_size, update_size)
        )
        own_upd, partner_upd = (whole_upd[0], whole_upd[1])
        own_rhs, partner_rhs = (whole_rhs[0], whole_rhs[1])
        out_rows, out_cols = (own_rows, own_cols)
        upper_half = leaf_index >> bit_no & 1 == 1
        first_upd = jnp.where(upper_half, partner_upd, own_upd)
        second_upd = jnp.where(upper_half, own_upd, partner_upd)
        first_rhs = jnp.where(upper_half, partner_rhs, own_rhs)
        second_rhs = jnp.where(upper_half, own_rhs, partner_rhs)
        front_id = offset + (leaf_index >> level_no)
        mapping = lax.dynamic_index_in_dim(child_rows, front_id, 0, keepdims=False)
        sep_coefs = lax.dynamic_index_in_dim(separator_coef, front_id, 0, keepdims=False)
        inv_first = inverse_map(mapping[0], front_size)
        inv_second = inverse_map(mapping[1], front_size)

        def assemble(parent_rows, parent_cols):
            return spread_block(first_upd, inv_first, parent_rows, parent_cols) + spread_block(
                second_upd, inv_second, parent_rows, parent_cols
            )

        diag_block = stencil_block(sep_coefs) + assemble(sep_rows, sep_rows)
        factor_inv = factor_inverse(diag_block)
        panel_rows = matmul_high(factor_inv, assemble(out_rows, sep_rows).T)
        panel_cols = matmul_high(factor_inv, assemble(out_cols, sep_rows).T)
        update_blk = assemble(out_rows, out_cols) - matmul_high(panel_rows.T, panel_cols)
        rhs_sep = spread_rows(first_rhs, inv_first, sep_rows) + spread_rows(
            second_rhs, inv_second, sep_rows
        )
        rhs_own = spread_rows(first_rhs, inv_first, out_rows) + spread_rows(
            second_rhs, inv_second, out_rows
        )
        solved = matmul_high(factor_inv, rhs_sep)
        rhs_blk = rhs_own - matmul_high(panel_rows.T, solved)
        store_here = leaf_index & (1 << level_no) - 1 == 1 << bit_no
        if level_no == levels:
            store_here = store_here | (leaf_index & (1 << bit_no) - 1 == 0)
        kept_rows = jnp.where(
            store_here,
            lax.dynamic_slice_in_dim(solved, row_index * sep_share, sep_share, 0),
            kept_rows,
        )
        offset += leaf_count >> level_no
    return (update_blk, rhs_blk, kept_rows[None])


def solution(mesh):
    in_specs = (P("leaf", "row", "col"), P("leaf", "row", "col"), P(), P())
    out_specs = (P("row", "col"), P("row", "col"), P("leaf", "row", "col"))
    return jax.shard_map(
        per_device, mesh=mesh, in_specs=in_specs, out_specs=out_specs, check_vma=False
    )
```

profile of v0, /device:TPU:56, one launch (start us, length us, event | category | flops | bytes accessed | tf_op | source)
XLA Modules:
  0.0 1204.7 jit_solution(3808599444853935362)
XLA Ops:
  7.2 3.4 collective-permute-start
  10.6 3.0 collective-permute-done
  21.3 3.0 scatter_custom_fusion.5
  35.0 27.5 %all-gather.11.cloned.1.call-done = f32[2,1024,256]{2,1,0:T(8,128)} async-done(((f32[2,64,256]{2,1,0:T(8,128)}), f32[2,1024,256]{2,1,0:T(8,128)}) %all-gather.11.cloned.1.call-update) | async-done | bytes 2097168 | tf_op jit(solution)/shard_map/all_gather | solution.py:92
  62.5 3.2 copy.566
  98.4 2.9 cholesky.1225
  129.8 2.9 cholesky.1269
  145.3 2.9 cholesky.1291
  177.8 3.1 cholesky.1335
  193.8 2.9 cholesky.1357
  224.9 4.9 collective-permute-start.1
  259.6 15.1 %all-gather.13.cloned.1.call-done = f32[2,1024,256]{2,1,0:T(8,128)} async-done(((f32[2,64,256]{2,1,0:T(8,128)}), f32[2,1024,256]{2,1,0:T(8,128)}) %all-gather.13.cloned.1.call-update) | async-done | bytes 2097168 | tf_op jit(solution)/shard_map/all_gather | solution.py:92
  310.6 2.9 cholesky.1401
  342.1 2.9 cholesky.1445
  357.7 2.9 cholesky.1467
  375.4 2.9 cholesky.1489
  391.0 3.1 cholesky.1511
  407.1 2.9 cholesky.1533
  438.1 3.4 collective-permute-start.2
  445.0 3.4 collective-permute-start.5
  482.3 4.1 all-gather.15.cloned.1.call-done
  522.7 2.9 cholesky.1577
  554.7 2.9 cholesky.1621
  604.1 3.1 cholesky.1687
  620.4 2.9 cholesky.1709
  651.4 4.2 collective-permute-start.3
  656.2 3.6 collective-permute-done.3
  674.3 26.1 %all_gather.35 = f32[2,512,128]{2,1,0:T(8,128)S(1)} all-gather(f32[2,64,128]{2,1,0:T(8,128)S(1)} %pad_maximum_fusion.5), channel_id=1, replica_groups=mesh['leaf'=32,'row'=8,'col'=2] {'row'}, dimensions={1}, use_global_device_ids=true | all-gather | bytes 589824 | tf_op jit(solution)/shard_map/all_gather | solution.py:95
  706.8 5.2 collective-permute-start.6
  747.3 2.9 cholesky.1753
  811.8 2.9 cholesky.1841
  827.4 3.3 cholesky.1863
  843.6 2.9 cholesky.1885
  874.3 5.0 collective-permute-start.4
  880.2 4.4 collective-permute-done.4
  885.2 26.0 %all_gather.36 = f32[2,512,128]{2,1,0:T(8,128)S(1)} all-gather(f32[2,64,128]{2,1,0:T(8,128)S(1)} %pad_maximum_fusion.6), channel_id=1, replica_groups=mesh['leaf'=32,'row'=8,'col'=2] {'row'}, dimensions={1}, use_global_device_ids=true | all-gather | bytes 589824 | tf_op jit(solution)/shard_map/all_gather | solution.py:95
  918.6 3.9 collective-permute-done.7
  922.4 25.7 %all_gather.37 = f32[2,512,128]{2,1,0:T(8,128)S(1)} all-gather(f32[2,64,128]{2,1,0:T(8,128)S(1)} %pad_maximum_fusion.7), channel_id=1, replica_groups=mesh['leaf'=32,'row'=8,'col'=2] {'row'}, dimensions={1}, use_global_device_ids=true | all-gather | bytes 589824 | tf_op jit(solution)/shard_map/all_gather | solution.py:95
  953.6 3.2 collective-permute-start.8
  956.8 3.5 collective-permute-done.8
  960.3 25.3 %all_gather.38 = f32[2,512,128]{2,1,0:T(8,128)S(1)} all-gather(f32[2,64,128]{2,1,0:T(8,128)S(1)} %pad_maximum_fusion.8), channel_id=1, replica_groups=mesh['leaf'=32,'row'=8,'col'=2] {'row'}, dimensions={1}, use_global_device_ids=true | all-gather | bytes 589824 | tf_op jit(solution)/shard_map/all_gather | solution.py:95
  991.2 5.0 collective-permute-start.9
  996.3 5.0 collective-permute-done.9
  1001.3 25.2 %all_gather.39 = f32[2,512,128]{2,1,0:T(8,128)S(1)} all-gather(f32[2,64,128]{2,1,0:T(8,128)S(1)} %pad_maximum_fusion.9), channel_id=1, replica_groups=mesh['leaf'=32,'row'=8,'col'=2] {'row'}, dimensions={1}, use_global_device_ids=true | all-gather | bytes 589824 | tf_op jit(solution)/shard_map/all_gather | solution.py:95
  1099.1 2.9 cholesky.1973
  1114.6 2.9 cholesky.1995
  1147.1 3.1 cholesky.2039
  1163.1 2.9 cholesky.2061
  (1930 shorter events, 870.5 us)
Async XLA Ops:
  7.2 55.3 %all-gather.11.cloned.1.call-start = ((), (), s32[]{:S(2)}) async-start(), calls=%async_computation | async-start | bytes 2228224 | tf_op jit(solution)/shard_map/all_gather | solution.py:92
  7.2 6.4 collective-permute-start
  15.1 259.6 %all-gather.13.cloned.1.call-start = ((), (), s32[]{:S(2)}) async-start(), calls=%async_computation.1 | async-start | bytes 2228224 | tf_op jit(solution)/shard_map/all_gather | solution.py:92
  31.0 180.8 %copy-start.89 = (s32[1024]{0:T(1024)}, s32[1024]{0:T(1024)S(1)}, u32[]{:S(2)}) copy-start(s32[1024]{0:T(1024)S(1)} %pad_clamp_fusion.24) | copy-start | bytes 12292
  31.7 178.2 %copy-start.91 = (s32[1024]{0:T(1024)}, s32[1024]{0:T(1024)S(1)}, u32[]{:S(2)}) copy-start(s32[1024]{0:T(1024)S(1)} %pad_clamp_fusion.25) | copy-start | bytes 12292
  31.7 35.0 %copy-start.144 = (s32[1024]{0:T(1024)}, s32[1024]{0:T(1024)S(1)}, u32[]{:S(2)}) copy-start(s32[1024]{0:T(1024)S(1)} %pad_clamp_fusion.30) | copy-start | bytes 12292
  33.8 33.6 %copy-start.198 = (pred[64]{0:T(512)(128)(4,1)}, pred[64]{0:T(512)(128)(4,1)S(1)}, u32[]{:S(2)}) copy-start(pred[64]{0:T(512)(128)(4,1)S(1)} %get-tuple-element.167) | copy-start | bytes 196
  153.0 69.9 %copy-start.25 = (f32[256,256]{1,0:T(8,128)}, f32[256,256]{1,0:T(8,128)S(1)}, u32[]{:S(2)}) copy-start(f32[256,256]{1,0:T(8,128)S(1)} %select_maximum_fusion.9) | copy-start | bytes 786436
  154.5 54.8 %copy-start.24 = (f32[256,64]{1,0:T(8,128)S(1)}, f32[256,64]{1,0:T(8,128)}, u32[]{:S(2)}) copy-start(f32[256,64]{1,0:T(8,128)} %gather_fusion.33) | copy-start | bytes 196612
  162.2 47.3 %copy-start = (f32[256,512]{1,0:T(8,128)S(1)}, f32[256,512]{1,0:T(8,128)}, u32[]{:S(2)}) copy-start(f32[256,512]{1,0:T(8,128)} %gather_fusion.40) | copy-start | bytes 1572868
  162.2 47.3 %copy-start.226 = (pred[256]{0:T(512)(128)(4,1)S(1)}, pred[256]{0:T(512)(128)(4,1)}, u32[]{:S(2)}) copy-start(pred[256]{0:T(512)(128)(4,1)} %get-tuple-element.143) | copy-start | bytes 772
  224.9 7.7 collective-permute-start.1
  233.2 253.1 %all-gather.15.cloned.1.call-start = ((), (), s32[]{:S(2)}) async-start(), calls=%async_computation.2 | async-start | bytes 2228224 | tf_op jit(solution)/shard_map/all_gather | solution.py:92
  251.9 24.5 %copy-start.132 = (s32[256]{0:T(256)}, s32[256]{0:T(256)S(1)}, u32[]{:S(2)}) copy-start(s32[256]{0:T(256)S(1)} %gather_fusion.5) | copy-start | bytes 3076
  255.9 169.2 %copy-start.93 = (s32[1024]{0:T(1024)}, s32[1024]{0:T(1024)S(1)}, u32[]{:S(2)}) copy-start(s32[1024]{0:T(1024)S(1)} %pad_clamp_fusion.18) | copy-start | bytes 12292
  257.2 24.2 %copy-start.95 = (s32[1024]{0:T(1024)}, s32[1024]{0:T(1024)S(1)}, u32[]{:S(2)}) copy-start(s32[1024]{0:T(1024)S(1)} %pad_clamp_fusion.19) | copy-start | bytes 12292
  365.4 70.8 %copy-start.27 = (f32[256,256]{1,0:T(8,128)}, f32[256,256]{1,0:T(8,128)S(1)}, u32[]{:S(2)}) copy-start(f32[256,256]{1,0:T(8,128)S(1)} %select_maximum_fusion.8) | copy-start | bytes 786436
  367.6 55.0 %copy-start.18 = (f32[256,64]{1,0:T(8,128)S(1)}, f32[256,64]{1,0:T(8,128)}, u32[]{:S(2)}) copy-start(f32[256,64]{1,0:T(8,128)} %gather_fusion.45) | copy-start | bytes 196612
  375.0 47.8 %copy-start.1 = (f32[256,512]{1,0:T(8,128)S(1)}, f32[256,512]{1,0:T(8,128)}, u32[]{:S(2)}) copy-start(f32[256,512]{1,0:T(8,128)} %gather_fusion.54) | copy-start | bytes 1572868
  375.0 47.8 %copy-start.223 = (pred[256]{0:T(512)(128)(4,1)S(1)}, pred[256]{0:T(512)(128)(4,1)}, u32[]{:S(2)}) copy-start(pred[256]{0:T(512)(128)(4,1)} %get-tuple-element.82) | copy-start | bytes 772
  438.1 6.2 collective-permute-start.2
  444.9 267.1 %all-gather.17.cloned.1.call-start = ((), (), s32[]{:S(2)}) async-start(), calls=%async_computation.3 | async-start | bytes 2228224 | tf_op jit(solution)/shard_map/all_gather | solution.py:92
  445.0 228.6 %collective-permute-start.5 = (f32[64,128]{1,0:T(8,128)}, f32[64,128]{1,0:T(8,128)}, u32[]{:S(2)}, u32[]{:S(2)}) collective-permute-start(f32[64,128]{1,0:T(8,128)} %bitcast.331), channel_id=1, source_target_pairs={{0,16},{16,0},{32,48},{48,32},{64,80},{80,64},{96,112},{112,96},{1... | collective-permute-start | bytes 98312 | tf_op jit(solution)/shard_map/ppermute | solution.py:14
  452.7 27.1 %copy-start.128 = (s32[256]{0:T(256)}, s32[256]{0:T(256)S(1)}, u32[]{:S(2)}) copy-start(s32[256]{0:T(256)S(1)} %gather_fusion.1) | copy-start | bytes 3076
  455.0 26.0 %copy-start.116 = (s32[512]{0:T(512)}, s32[512]{0:T(512)S(1)}, u32[]{:S(2)}) copy-start(s32[512]{0:T(512)S(1)} %gather_fusion.28) | copy-start | bytes 6148
  578.3 71.3 %copy-start.29 = (f32[256,256]{1,0:T(8,128)}, f32[256,256]{1,0:T(8,128)S(1)}, u32[]{:S(2)}) copy-start(f32[256,256]{1,0:T(8,128)S(1)} %select_maximum_fusion.7) | copy-start | bytes 786436
  580.5 55.6 %copy-start.19 = (f32[256,64]{1,0:T(8,128)S(1)}, f32[256,64]{1,0:T(8,128)}, u32[]{:S(2)}) copy-start(f32[256,64]{1,0:T(8,128)} %gather_fusion.59) | copy-start | bytes 196612
  587.9 48.3 %copy-start.2 = (f32[256,512]{1,0:T(8,128)S(1)}, f32[256,512]{1,0:T(8,128)}, u32[]{:S(2)}) copy-start(f32[256,512]{1,0:T(8,128)} %gather_fusion.68) | copy-start | bytes 1572868
  587.9 48.3 %copy-start.219 = (pred[256]{0:T(512)(128)(4,1)S(1)}, pred[256]{0:T(512)(128)(4,1)}, u32[]{:S(2)}) copy-start(pred[256]{0:T(512)(128)(4,1)} %get-tuple-element.145) | copy-start | bytes 772
  651.4 8.5 collective-permute-start.3
  660.5 371.8 %all-gather.19.cloned.1.call-start = ((), (), s32[]{:S(2)}) async-start(), calls=%async_computation.4 | async-start | bytes 2228224 | tf_op jit(solution)/shard_map/all_gather | solution.py:92
  664.1 37.0 %copy-start.92 = (s32[1024]{0:T(1024)S(1)}, s32[1024]{0:T(1024)}, u32[]{:S(2)}) copy-start(s32[1024]{0:T(1024)} %copy-done.91) | copy-start | bytes 12292
  670.0 48.1 %copy-start.108 = (s32[1024]{0:T(1024)}, s32[1024]{0:T(1024)S(1)}, u32[]{:S(2)}) copy-start(s32[1024]{0:T(1024)S(1)} %pad_clamp_fusion.7) | copy-start | bytes 12292
  670.6 44.7 %copy-start.214 = (pred[64]{0:T(512)(128)(4,1)}, pred[64]{0:T(512)(128)(4,1)S(1)}, u32[]{:S(2)}) copy-start(pred[64]{0:T(512)(128)(4,1)S(1)} %get-tuple-element.155) | copy-start | bytes 196
  673.5 41.1 %copy-start.147 = (s32[1024]{0:T(1024)}, s32[1024]{0:T(1024)S(1)}, u32[]{:S(2)}) copy-start(s32[1024]{0:T(1024)S(1)} %pad_clamp_fusion.11) | copy-start | bytes 12292
  706.8 172.6 %collective-permute-start.6 = (f32[64,128]{1,0:T(8,128)}, f32[64,128]{1,0:T(8,128)}, u32[]{:S(2)}, u32[]{:S(2)}) collective-permute-start(f32[64,128]{1,0:T(8,128)} %convolution_subtract_fusion.44), channel_id=1, source_target_pairs={{0,32},{32,0},{16,48},{48,16},{64,96},{96,64},{80,112},{112,80},{1... | collective-permute-start | bytes 98312 | tf_op jit(solution)/shard_map/ppermute | solution.py:14
  811.4 47.8 %copy-start.3 = (f32[256,512]{1,0:T(8,128)S(1)}, f32[256,512]{1,0:T(8,128)}, u32[]{:S(2)}) copy-start(f32[256,512]{1,0:T(8,128)} %gather_fusion.82) | copy-start | bytes 1572868
  811.4 47.8 %copy-start.221 = (pred[256]{0:T(512)(128)(4,1)S(1)}, pred[256]{0:T(512)(128)(4,1)}, u32[]{:S(2)}) copy-start(pred[256]{0:T(512)(128)(4,1)} %get-tuple-element.74) | copy-start | bytes 772
  873.9 38.0 %copy-start.98 = (s32[1024]{0:T(1024)S(1)}, s32[1024]{0:T(1024)}, u32[]{:S(2)}) copy-start(s32[1024]{0:T(1024)} %copy-done.95) | copy-start | bytes 12292
  874.3 10.2 collective-permute-start.4
  916.3 31.9 %copy-start.15 = (f32[512,128]{1,0:T(8,128)}, f32[512,128]{1,0:T(8,128)S(1)}, u32[]{:S(2)}) copy-start(f32[512,128]{1,0:T(8,128)S(1)} %fusion.306) | copy-start | bytes 786436
  916.3 32.6 %copy-start.106 = (s32[1024]{0:T(1024)S(1)}, s32[1024]{0:T(1024)}, u32[]{:S(2)}) copy-start(s32[1024]{0:T(1024)} %copy-done.103) | copy-start | bytes 12292
  916.6 5.8 collective-permute-start.7
  953.3 32.4 %copy-start.16 = (f32[512,128]{1,0:T(8,128)}, f32[512,128]{1,0:T(8,128)S(1)}, u32[]{:S(2)}) copy-start(f32[512,128]{1,0:T(8,128)S(1)} %fusion.303) | copy-start | bytes 786436
  953.6 6.8 collective-permute-start.8
  991.2 10.1 collective-permute-start.9
  1131.1 47.6 %copy-start.4 = (f32[256,512]{1,0:T(8,128)S(1)}, f32[256,512]{1,0:T(8,128)}, u32[]{:S(2)}) copy-start(f32[256,512]{1,0:T(8,128)} %gather_fusion.96) | copy-start | bytes 1572868
  1131.1 47.6 %copy-start.217 = (pred[256]{0:T(512)(128)(4,1)S(1)}, pred[256]{0:T(512)(128)(4,1)}, u32[]{:S(2)}) copy-start(pred[256]{0:T(512)(128)(4,1)} %get-tuple-element.147) | copy-start | bytes 772
  (237 other events, 1089.9 us)
Sparse Core Ops, SparseCore 0:
  15.2 47.2 all-gather.10
  233.4 41.2 all-gather.12
  445.0 41.2 all-gather.14
  660.7 42.0 all-gather.16
  885.3 39.5 all-gather.18
where the time goes:
time: 1210 us; the launch traced here: 1200 us
  other arithmetic  596 us (49%)
  local copies, waits for them, and re-layouts  231 us (19%)
  blocking collectives  128 us (11%)
  matrix products  110 us (9%)
  waiting for transfers between devices  75.7 us (6%)
  starting transfers between devices  39.8 us (3%)
  between operations  23.6 us (2%)
    another operation x240, other arithmetic, factor_inverse(): lower_factor = jnp.linalg.cholesky(matrix)  291 us
    another operation x160, other arithmetic, factor_inverse(): return jax.scipy.linalg.solve_triangular(lower_factor, identity, lower=True)  247 us
    all_gather x5, blocking collectives, per_device(): lax.all_gather(jnp.stack([rhs_blk, other_rhs]), 'row', axis=1, tiled=True)  128 us
    dot_general x325, matrix products, matmul_high(): return jnp.dot(left, right, precision=lax.Precision.HIGHEST)  91 us
    gather x50, local copies, waits for them, and re-layouts, spread_block(): jnp.take(jnp.take(full_matrix, jnp.maximum(src_rows, 0), axis=0), jnp.max...  60.6 us
    all_gather x5, waiting for transfers between devices, per_device(): lax.all_gather(jnp.stack([update_blk, other_upd])[:, None], ('row', 'col'...  46.7 us
    gather x30, local copies, waits for them, and re-layouts, spread_block(): jnp.take(full_matrix, jnp.maximum(src_rows, 0), axis=0)  41.8 us
    ppermute x10, starting transfers between devices, from_partner(): return lax.ppermute(block, axis, route)  39.6 us
  transfers between devices with their start and end apart: 15, of which 11 were waited for; matrix products, arithmetic and copies ran while one was open for 37% of the time, Pallas kernels for 0%

commit v1 on v0

--- a/solution.py
+++ b/solution.py
@@ -92,7 +92,9 @@
         blocks = lax.all_gather(
             jnp.stack([update_blk, other_upd])[:, None], ("row", "col"), axis=1, tiled=True
         )
-        whole_rhs = lax.all_gather(jnp.stack([rhs_blk, other_rhs]), "row", axis=1, tiled=True)
+        array = jnp.stack([rhs_blk, other_rhs])
+        copies = jnp.concatenate([array] * lax.axis_size("row"), axis=1)
+        whole_rhs = lax.all_to_all(copies, "row", 1, 1, tiled=True)
         whole_upd = (
             blocks.reshape(2, row_count, col_count, row_block, col_block)
             .transpose(0, 1, 3, 2, 4)

time: 1210 us -> 1130 us (0.934)
  blocking collectives: 128 us -> 0 us
  starting transfers between devices: 39.8 us -> 68.7 us
  waiting for transfers between devices: 75.7 us -> 90.7 us
    all_gather x5 -> x0, blocking collectives: 128 us -> none  [per_device(): lax.all_gather(jnp.stack([rhs_blk, other_rhs]), 'row', axis=1, tiled=True)]
    all_to_all x0 -> x5, waiting for transfers between devices: none -> 40.7 us  [per_device(): whole_rhs = lax.all_to_all(copies, 'row', 1, 1, tiled=True)]
    all_to_all x0 -> x5, starting transfers between devices: none -> 29 us  [per_device(): whole_rhs = lax.all_to_all(copies, 'row', 1, 1, tiled=True)]
    all_gather x5, waiting for transfers between devices: 46.7 us -> 27.4 us  [per_device(): lax.all_gather(jnp.stack([update_blk, other_upd])[:, None], ('row', 'col'...]
  transfers between devices with their start and end apart: 15 -> 20, of which waited for: 11 -> 12; matrix products, arithmetic and copies ran while one was open for 37% -> 55% of each run, Pallas kernels for 0% -> 0%
where the time goes in v1:
time: 1130 us; the launch traced here: 1110 us
  other arithmetic  589 us (52%)
  local copies, waits for them, and re-layouts  231 us (20%)
  matrix products  110 us (10%)
  waiting for transfers between devices  90.7 us (8%)
  starting transfers between devices  68.7 us (6%)
  between operations  23.7 us (2%)
    another operation x240, other arithmetic, factor_inverse(): lower_factor = jnp.linalg.cholesky(matrix)  289 us
    another operation x160, other arithmetic, factor_inverse(): return jax.scipy.linalg.solve_triangular(lower_factor, identity, lower=True)  245 us
    dot_general x325, matrix products, matmul_high(): return jnp.dot(left, right, precision=lax.Precision.HIGHEST)  91.1 us
    gather x50, local copies, waits for them, and re-layouts, spread_block(): jnp.take(jnp.take(full_matrix, jnp.maximum(src_rows, 0), axis=0), jnp.max...  60.9 us
    all_to_all x5, waiting for transfers between devices, per_device(): whole_rhs = lax.all_to_all(copies, 'row', 1, 1, tiled=True)  40.7 us
    gather x30, local copies, waits for them, and re-layouts, spread_block(): jnp.take(full_matrix, jnp.maximum(src_rows, 0), axis=0)  39.4 us
    ppermute x10, starting transfers between devices, from_partner(): return lax.ppermute(block, axis, route)  39.3 us
    gather x20, local copies, waits for them, and re-layouts, spread_block(): src_rows = inverse[parent_rows]  33.8 us
  transfers between devices with their start and end apart: 20, of which 12 were waited for; matrix products, arithmetic and copies ran while one was open for 55% of the time, Pallas kernels for 0%

profile of v1, /device:TPU:56, one launch (start us, length us, event | category | flops | bytes accessed | tf_op | source)
XLA Modules:
  0.0 1113.6 jit_solution(13924587151832242701)
XLA Ops:
  7.2 3.4 collective-permute-start
  10.6 3.0 collective-permute-done
  15.2 3.4 collective-permute-start.5
  82.6 3.2 copy.820
  114.6 2.9 cholesky.1225
  146.1 2.9 cholesky.1269
  161.6 2.9 cholesky.1291
  195.4 3.1 cholesky.1335
  211.5 2.9 cholesky.1357
  242.5 4.6 collective-permute-start.1
  247.1 3.0 collective-permute-done.1
  263.4 10.3 all-to-all-start
  274.0 27.4 %all-gather.13.cloned.1.call-done = f32[2,1024,256]{2,1,0:T(8,128)} async-done(((f32[2,64,256]{2,1,0:T(8,128)}), f32[2,1024,256]{2,1,0:T(8,128)}) %all-gather.13.cloned.1.call-update) | async-done | bytes 2097168 | tf_op jit(solution)/shard_map/all_gather | solution.py:92
  332.3 2.9 cholesky.1401
  363.8 2.9 cholesky.1445
  379.4 2.9 cholesky.1467
  396.2 2.9 cholesky.1489
  411.8 3.1 cholesky.1511
  427.9 2.9 cholesky.1533
  458.8 3.7 collective-permute-start.2
  474.5 5.5 collective-permute-start.6
  483.1 4.2 all-to-all-start.1
  492.8 14.5 %all-to-all-done.1 = f32[2,512,128]{2,0,1:T(2,128)S(1)} async-done(((f32[2,512,128]{2,0,1:T(2,128)}), f32[2,512,128]{2,0,1:T(2,128)S(1)}, u32[]{:S(2)}, u32[]{:S(2)}) %all-to-all-start.1) | async-done | bytes 524320 | tf_op jit(solution)/shard_map/all_to_all | solution.py:97
  546.0 2.9 cholesky.1577
  576.9 2.9 cholesky.1621
  592.2 2.9 cholesky.1643
  608.8 2.9 cholesky.1665
  624.1 3.1 cholesky.1687
  670.5 4.4 collective-permute-start.3
  675.3 3.1 collective-permute-start.7
  682.4 3.5 all-to-all-start.2
  694.4 9.2 all-to-all-done.2
  712.6 4.0 collective-permute-done.8
  717.9 4.1 all-to-all-start.3
  749.0 2.9 cholesky.1753
  780.4 2.9 cholesky.1797
  796.0 2.9 cholesky.1819
  829.8 3.3 cholesky.1863
  846.1 2.9 cholesky.1885
  885.5 4.7 collective-permute-start.4
  903.7 4.0 collective-permute-start.9
  907.7 6.0 collective-permute-done.9
  915.0 6.8 all-to-all-start.4
  922.5 16.9 %all-to-all-done.4 = f32[2,512,128]{2,0,1:T(2,128)S(1)} async-done(((f32[2,512,128]{2,0,1:T(2,128)}), f32[2,512,128]{2,0,1:T(2,128)S(1)}, u32[]{:S(2)}, u32[]{:S(2)}) %all-to-all-start.4) | async-done | bytes 524320 | tf_op jit(solution)/shard_map/all_to_all | solution.py:97
  1023.2 2.9 cholesky.1995
  1040.1 2.9 cholesky.2017
  1055.6 3.2 cholesky.2039
  1071.7 2.9 cholesky.2061
  (1907 shorter events, 862.7 us)
Async XLA Ops:
  7.2 75.4 %all-gather.11.cloned.1.call-start = ((), (), s32[]{:S(2)}) async-start(), calls=%async_computation.5 | async-start | bytes 2228224 | tf_op jit(solution)/shard_map/all_gather | solution.py:92
  7.2 6.4 collective-permute-start
  15.1 286.3 %all-gather.13.cloned.1.call-start = ((), (), s32[]{:S(2)}) async-start(), calls=%async_computation.6 | async-start | bytes 2228224 | tf_op jit(solution)/shard_map/all_gather | solution.py:92
  15.2 242.8 %collective-permute-start.5 = (f32[64,128]{1,0:T(8,128)}, f32[64,128]{1,0:T(8,128)S(1)}, u32[]{:S(2)}, u32[]{:S(2)}) collective-permute-start(f32[64,128]{1,0:T(8,128)} %bitcast.1665), channel_id=1, source_target_pairs={{0,16},{16,0},{32,48},{48,32},{64,80},{80,64},{96,112},{112,96},{1... | collective-permute-start | bytes 98312 | tf_op jit(solution)/shard_map/ppermute | solution.py:14
  22.5 49.3 %copy-start.67 = (s32[1024]{0:T(1024)}, s32[1024]{0:T(1024)S(1)}, u32[]{:S(2)}) copy-start(s32[1024]{0:T(1024)S(1)} %pad_clamp_fusion.32) | copy-start | bytes 12292
  23.3 49.3 %copy-start.65 = (s32[1024]{0:T(1024)}, s32[1024]{0:T(1024)S(1)}, u32[]{:S(2)}) copy-start(s32[1024]{0:T(1024)S(1)} %pad_clamp_fusion.31) | copy-start | bytes 12292
  29.8 46.5 %copy-start.32 = (s32[1024]{0:T(1024)}, s32[1024]{0:T(1024)S(1)}, u32[]{:S(2)}) copy-start(s32[1024]{0:T(1024)S(1)} %pad_clamp_fusion.26) | copy-start | bytes 12292
  41.7 215.6 %copy-start.72 = (s32[512]{0:T(512)}, s32[512]{0:T(512)S(1)}, u32[]{:S(2)}) copy-start(s32[512]{0:T(512)S(1)} %gather_fusion.20) | copy-start | bytes 6148
  46.9 209.3 %copy-start.79 = (s32[256]{0:T(256)}, s32[256]{0:T(256)S(1)}, u32[]{:S(2)}) copy-start(s32[256]{0:T(256)S(1)} %gather_fusion.3) | copy-start | bytes 3076
  56.6 200.7 %copy-start.74 = (s32[512]{0:T(512)}, s32[512]{0:T(512)S(1)}, u32[]{:S(2)}) copy-start(s32[512]{0:T(512)S(1)} %gather_fusion.21) | copy-start | bytes 6148
  61.7 194.5 %copy-start.81 = (s32[256]{0:T(256)}, s32[256]{0:T(256)S(1)}, u32[]{:S(2)}) copy-start(s32[256]{0:T(256)S(1)} %gather_fusion.23) | copy-start | bytes 3076
  78.7 148.9 %copy-start.57 = (s32[1024]{0:T(1024)}, s32[1024]{0:T(1024)S(1)}, u32[]{:S(2)}) copy-start(s32[1024]{0:T(1024)S(1)} %pad_clamp_fusion.25) | copy-start | bytes 12292
  82.0 158.5 %copy-start.99 = (pred[512]{0:T(512)(128)(4,1)}, pred[512]{0:T(512)(128)(4,1)S(1)}, u32[]{:S(2)}) copy-start(pred[512]{0:T(512)(128)(4,1)S(1)} %get-tuple-element.77) | copy-start | bytes 1540
  82.0 158.5 %copy-start.101 = (pred[512]{0:T(512)(128)(4,1)}, pred[512]{0:T(512)(128)(4,1)S(1)}, u32[]{:S(2)}) copy-start(pred[512]{0:T(512)(128)(4,1)S(1)} %get-tuple-element.78) | copy-start | bytes 1540
  172.2 54.8 %copy-start.20 = (f32[256,64]{1,0:T(8,128)S(1)}, f32[256,64]{1,0:T(8,128)}, u32[]{:S(2)}) copy-start(f32[256,64]{1,0:T(8,128)} %gather_fusion.33) | copy-start | bytes 196612
  179.5 47.6 %copy-start.15 = (f32[256,64]{1,0:T(8,128)S(1)}, f32[256,64]{1,0:T(8,128)}, u32[]{:S(2)}) copy-start(f32[256,64]{1,0:T(8,128)} %gather_fusion.31) | copy-start | bytes 196612
  179.9 47.3 %copy-start = (f32[256,512]{1,0:T(8,128)S(1)}, f32[256,512]{1,0:T(8,128)}, u32[]{:S(2)}) copy-start(f32[256,512]{1,0:T(8,128)} %gather_fusion.40) | copy-start | bytes 1572868
  179.9 47.3 %copy-start.175 = (pred[256]{0:T(512)(128)(4,1)S(1)}, pred[256]{0:T(512)(128)(4,1)}, u32[]{:S(2)}) copy-start(pred[256]{0:T(512)(128)(4,1)} %get-tuple-element.153) | copy-start | bytes 772
  242.1 61.0 %copy-start.9 = (f32[512,64]{0,1:T(8,128)}, f32[512,64]{0,1:T(8,128)S(1)}, u32[]{:S(2)}) copy-start(f32[512,64]{0,1:T(8,128)S(1)} %fusion.294) | copy-start | bytes 393220
  242.5 7.7 collective-permute-start.1
  252.0 191.8 %copy-start.60 = (s32[1024]{0:T(1024)}, s32[1024]{0:T(1024)S(1)}, u32[]{:S(2)}) copy-start(s32[1024]{0:T(1024)S(1)} %pad_clamp_fusion.19) | copy-start | bytes 12292
  253.8 50.9 %copy-start.154 = (pred[64]{0:T(512)(128)(4,1)}, pred[64]{0:T(512)(128)(4,1)S(1)}, u32[]{:S(2)}) copy-start(pred[64]{0:T(512)(128)(4,1)S(1)} %get-tuple-element.112) | copy-start | bytes 196
  258.0 46.0 %copy-start.96 = (s32[1024]{0:T(1024)}, s32[1024]{0:T(1024)S(1)}, u32[]{:S(2)}) copy-start(s32[1024]{0:T(1024)S(1)} %pad_clamp_fusion.23) | copy-start | bytes 12292
  263.4 203.5 %all-to-all-start = ((f32[2,512,128]{2,0,1:T(2,128)}), f32[2,512,128]{2,0,1:T(2,128)}, u32[]{:S(2)}, u32[]{:S(2)}) async-start(f32[2,512,128]{2,0,1:T(2,128)} %constant_dynamic-update-slice_fusion), calls=%async_computation | async-start | bytes 1048576 | tf_op jit(solution)/shard_map/all_to_all | solution.py:97
  273.7 240.7 %all-gather.15.cloned.1.call-start = ((), (), s32[]{:S(2)}) async-start(), calls=%async_computation.7 | async-start | bytes 2228224 | tf_op jit(solution)/shard_map/all_gather | solution.py:92
  395.8 47.7 %copy-start.1 = (f32[256,512]{1,0:T(8,128)S(1)}, f32[256,512]{1,0:T(8,128)}, u32[]{:S(2)}) copy-start(f32[256,512]{1,0:T(8,128)} %gather_fusion.54) | copy-start | bytes 1572868
  395.9 47.6 %copy-start.173 = (pred[256]{0:T(512)(128)(4,1)S(1)}, pred[256]{0:T(512)(128)(4,1)}, u32[]{:S(2)}) copy-start(pred[256]{0:T(512)(128)(4,1)} %get-tuple-element.92) | copy-start | bytes 772
  458.8 6.2 collective-permute-start.2
  474.5 7.4 collective-permute-start.6
  483.1 24.2 %all-to-all-start.1 = ((f32[2,512,128]{2,0,1:T(2,128)}), f32[2,512,128]{2,0,1:T(2,128)S(1)}, u32[]{:S(2)}, u32[]{:S(2)}) async-start(f32[2,512,128]{2,0,1:T(2,128)} %copy.697), calls=%async_computation.1 | async-start | bytes 1048576 | tf_op jit(solution)/shard_map/all_to_all | solution.py:97
  487.4 234.7 %all-gather.17.cloned.1.call-start = ((), (), s32[]{:S(2)}) async-start(), calls=%async_computation.8 | async-start | bytes 2228224 | tf_op jit(solution)/shard_map/all_gather | solution.py:92
  601.3 53.9 %copy-start.16 = (f32[256,64]{1,0:T(8,128)S(1)}, f32[256,64]{1,0:T(8,128)}, u32[]{:S(2)}) copy-start(f32[256,64]{1,0:T(8,128)} %gather_fusion.59) | copy-start | bytes 196612
  608.4 46.8 %copy-start.2 = (f32[256,512]{1,0:T(8,128)S(1)}, f32[256,512]{1,0:T(8,128)}, u32[]{:S(2)}) copy-start(f32[256,512]{1,0:T(8,128)} %gather_fusion.68) | copy-start | bytes 1572868
  608.5 46.8 %copy-start.168 = (pred[256]{0:T(512)(128)(4,1)S(1)}, pred[256]{0:T(512)(128)(4,1)}, u32[]{:S(2)}) copy-start(pred[256]{0:T(512)(128)(4,1)} %get-tuple-element.155) | copy-start | bytes 772
  670.5 7.8 collective-permute-start.3
  675.3 5.8 collective-permute-start.7
  682.4 21.2 %all-to-all-start.2 = ((f32[2,512,128]{2,0,1:T(2,128)}), f32[2,512,128]{2,0,1:T(2,128)S(1)}, u32[]{:S(2)}, u32[]{:S(2)}) async-start(f32[2,512,128]{2,0,1:T(2,128)} %copy.700), calls=%async_computation.2 | async-start | bytes 1048576 | tf_op jit(solution)/shard_map/all_to_all | solution.py:97
  694.4 44.7 %copy-start.129 = (pred[512]{0:T(512)(128)(4,1)}, pred[512]{0:T(512)(128)(4,1)S(1)}, u32[]{:S(2)}) copy-start(pred[512]{0:T(512)(128)(4,1)S(1)} %get-tuple-element.66) | copy-start | bytes 1540
  694.4 44.7 %copy-start.131 = (pred[512]{0:T(512)(128)(4,1)}, pred[512]{0:T(512)(128)(4,1)S(1)}, u32[]{:S(2)}) copy-start(pred[512]{0:T(512)(128)(4,1)S(1)} %get-tuple-element.125) | copy-start | bytes 1540
  694.4 44.6 %copy-start.134 = (pred[512]{0:T(512)(128)(4,1)}, pred[512]{0:T(512)(128)(4,1)S(1)}, u32[]{:S(2)}) copy-start(pred[512]{0:T(512)(128)(4,1)S(1)} %get-tuple-element.126) | copy-start | bytes 1540
  709.9 6.7 collective-permute-start.8
  717.9 179.1 %all-to-all-start.3 = ((f32[2,512,128]{2,0,1:T(2,128)}), f32[2,512,128]{2,0,1:T(2,128)}, u32[]{:S(2)}, u32[]{:S(2)}) async-start(f32[2,512,128]{2,0,1:T(2,128)} %copy.703), calls=%async_computation.3 | async-start | bytes 1048576 | tf_op jit(solution)/shard_map/all_to_all | solution.py:97
  722.1 223.5 %all-gather.19.cloned.1.call-start = ((), (), s32[]{:S(2)}) async-start(), calls=%async_computation.9 | async-start | bytes 2228224 | tf_op jit(solution)/shard_map/all_gather | solution.py:92
  885.5 10.8 collective-permute-start.4
  903.7 10.0 collective-permute-start.9
  915.0 24.4 %all-to-all-start.4 = ((f32[2,512,128]{2,0,1:T(2,128)}), f32[2,512,128]{2,0,1:T(2,128)S(1)}, u32[]{:S(2)}, u32[]{:S(2)}) async-start(f32[2,512,128]{2,0,1:T(2,128)} %copy.706), calls=%async_computation.4 | async-start | bytes 1048576 | tf_op jit(solution)/shard_map/all_to_all | solution.py:97
  1039.7 47.6 %copy-start.3 = (f32[256,512]{1,0:T(8,128)S(1)}, f32[256,512]{1,0:T(8,128)}, u32[]{:S(2)}) copy-start(f32[256,512]{1,0:T(8,128)} %gather_fusion.96) | copy-start | bytes 1572868
  1039.7 47.6 %copy-start.165 = (pred[256]{0:T(512)(128)(4,1)S(1)}, pred[256]{0:T(512)(128)(4,1)}, u32[]{:S(2)}) copy-start(pred[256]{0:T(512)(128)(4,1)} %get-tuple-element.157) | copy-start | bytes 772
  (206 other events, 1382.8 us)
Sparse Core Ops, SparseCore 0:
  15.2 47.2 all-gather.10
  250.9 50.4 all-gather.12
  465.8 44.9 all-gather.14
  679.1 42.0 all-gather.16
  897.1 45.9 all-gather.18
